TPU v7x, 32 devices: a whole 2x2x4 slice. The times are simulated.
32 devices in a mesh: node: 16 (over z, x, core), feat: 2 (over y).
Axes of the slice: x: 2, y: 2, z: 4, core: 2. Of those that a mesh axis runs over, the one named last changes fastest.
Arguments:
- covariates: bfloat16 [256, 65536], P('feat', 'node'), may hold values from 0 to 0.9921875
- pseudo: bfloat16 [16, 65536], P(None, 'node'), may hold values from -6 to 6
- honest: int32 [65536], P('node'), may hold values 0 or 1
- destination: int32 [65536, 1], P('node'), may hold values from 0 to 31; in each aligned block of 4096 rows (0 to 4095, 4096 to 8191, ...) at most 256 rows name the same one
- node_slot: int32 [32], replicated, may hold values from 0 to 31, each once
Outputs:
- histogram: float32 [32, 256, 17, 256], P('node', 'feat')
- best_gain: float32 [32], P('node')
Inputs may be any that keep to these rules, and one draw needn't show every extreme that they name: `destination`: in the rows of one device no child node is named by more than 256 rows. Each slot appears once; child node n belongs to the owner node_slot[n] // 2 along node.
All inputs are finite; a program needn't handle non-finite values. No bound on the sum of `honest` on one device may be relied on, other than what follows from the above.
Results may differ from a plain program's by a relative error of at most 0.0003.
Values may be sent and summed in bfloat16 or wider, within the bound.
A program may use at most 64 MiB of HBM per device.

v0:
```python
import jax
import jax.numpy as jnp
from jax import lax
from jax.sharding import PartitionSpec as P

B = 256


def feature_histograms(bin_table, statistics):
    levels = lax.broadcasted_iota(jnp.int32, (1, 1, B), 2)

    def one_feature(bin_row):
        indicator = (bin_row[:, :, None] == levels).astype(jnp.bfloat16)
        return jnp.einsum("skr,krb->ksb", statistics, indicator, preferred_element_type=jnp.float32)

    stacked = lax.map(one_feature, bin_table)
    return jnp.transpose(stacked, (1, 0, 2, 3))


def on_device(covariates, pseudo, honest, destination, node_slot):
    feat_count, row_count = covariates.shape
    node_devices = lax.axis_size("node")
    node_total = node_slot.shape[0]
    node_local = node_total // node_devices
    capacity = 2 * row_count // node_total
    weight = (1 - honest).astype(jnp.float32)
    columns = lax.broadcasted_iota(jnp.int32, (1, node_total), 1)
    named = (destination == columns).astype(jnp.int32)
    target = jnp.sum(named * node_slot[None, :], axis=1)
    owned = (target[:, None] == columns).astype(jnp.int32)
    rank = jnp.sum((jnp.cumsum(owned, axis=0) - 1) * owned, axis=1)
    position = target * capacity + rank
    weighted = weight[None, :] * pseudo.astype(jnp.float32)
    weight_row = weight[None, :].astype(jnp.bfloat16)
    payload = jnp.concatenate([covariates, weight_row, weighted.astype(jnp.bfloat16)], axis=0)
    payload_width = payload.shape[0]
    outgoing = (
        jnp.zeros((payload_width, node_total * capacity), jnp.bfloat16).at[:, position].set(payload)
    )
    outgoing = outgoing.reshape(payload_width, node_devices, node_local, capacity)
    arrived = lax.all_to_all(outgoing, "node", split_axis=1, concat_axis=3, tiled=True)[:, 0]
    bin_table = jnp.floor(arrived[:feat_count].astype(jnp.float32) * B).astype(jnp.int32)
    statistics = arrived[feat_count:]
    histogram = feature_histograms(bin_table, statistics)
    left = jnp.cumsum(histogram, axis=3)
    total = left[:, :, :, -1:]
    right = total - left
    left_part = jnp.sum(left[:, :, 1:] * left[:, :, 1:], axis=2) / (left[:, :, 0] + 1.0)
    right_part = jnp.sum(right[:, :, 1:] * right[:, :, 1:], axis=2) / (right[:, :, 0] + 1.0)
    total_part = jnp.sum(total[:, :, 1:] * total[:, :, 1:], axis=2) / (total[:, :, 0] + 1.0)
    gain = left_part + right_part - total_part
    best_local = jnp.max(gain, axis=(1, 2))
    best_gain = lax.pmax(best_local, "feat")
    return (histogram, best_gain)


def solution(mesh):
    placed = (P("feat", "node"), P(None, "node"), P("node"), P("node", None), P())
    return jax.shard_map(
        on_device,
        mesh=mesh,
        in_specs=placed,
        out_specs=(P("node", "feat", None, None), P("node")),
        check_vma=False,
    )
```

profile of v0, /device:TPU:20, one launch (start us, length us, event | category | flops | bytes accessed | tf_op | source)
XLA Modules:
  0.0 692.2 jit_solution(4010520840536769933)
XLA Ops:
  2.4 9.2 %reduce-window.14 = s32[32,32,128]{2,1,0:T(8,128)S(1)} reduce-window(s32[32,32,128]{2,1,0:T(8,128)S(1)} %fusion.11, s32[]{:T(128)} %constant.16.clone.1), window={size=1x1x128 pad=0_0x0_0x127_0}, to_apply=%region_1.0 | reduce-window | flops 16646144 | bytes 1048580 | tf_op jit(solution)/shard_map/reduce-window
  14.3 1.9 copy.35
  16.2 20.6 %scatter_custom_fusion = bf16[145,8192]{0,1:T(8,128)(2,1)} fusion(s32[4096]{0:T(1024)S(1)} %bitcast.107, bf16[4096,145]{1,0:T(8,128)(2,1)S(1)} %copy.35, bf16[]{:T(256)} %constant.18.clone.1), kind=kCustom, calls=%fused_computation.14 | custom fusion | bytes 2375682 | tf_op jit(solution)/shard_map/scatter | solution.py:38
  36.8 9.1 %copy.36 = bf16[145,16,2,256]{3,2,0,1:T(2,128)(2,1)} copy(bf16[145,16,2,256]{0,3,2,1:T(8,128)(2,1)} %bitcast.96) | data formatting | bytes 4751360 | tf_op jit(solution)/shard_map/reshape | solution.py:40
  45.9 6.2 all-to-all-start
  52.0 53.6 %all-to-all-done = bf16[145,16,2,256]{3,2,0,1:T(2,128)(2,1)S(1)} async-done(((bf16[145,16,2,256]{3,2,0,1:T(2,128)(2,1)}), bf16[145,16,2,256]{3,2,0,1:T(2,128)(2,1)S(1)}, u32[]{:S(2)}, u32[]{:S(2)}) %all-to-all-start) | async-done | bytes 2375712 | tf_op jit(solution)/shard_map/all_to_all | solution.py:41
  105.6 8.7 %copy.37 = bf16[145,16,2,256]{0,3,1,2:T(8,128)(2,1)} copy(bf16[145,16,2,256]{3,2,0,1:T(2,128)(2,1)S(1)} %all-to-all-done) | data formatting | bytes 4751360 | tf_op jit(solution)/shard_map/all_to_all | solution.py:41
  114.4 1.9 slice.65
  117.2 2.7 floor_convert_fusion
  119.9 7.3 %copy.39 = s32[128,2,4096]{2,1,0:T(2,128)} copy(s32[128,2,4096]{0,2,1:T(8,128)} %bitcast.97) | data formatting | bytes 8388608
  128.1 538.5 %while.11 = (s32[]{:T(128)}, f32[128,2,17,256]{3,0,2,1:T(8,128)}, s32[128,2,4096]{2,1,0:T(2,128)}, bf16[17,2,4096]{2,0,1:T(8,128)(2,1)S(1)}, s32[]{:T(128)}, /*index=5*/s32[]{:T(128)}) while((s32[]{:T(128)}, f32[128,2,17,256]{3,0,2,1:T(8,128)}, s32[128,2,4096]{2,1,0:T(2,128)}, bf16[17,2,4096]{2,0,1:T(8,128)(2,1)S(1)}, s32[]{:T(128)}, ...), condition=%wide.region_6.7_spmd.clone, body=%wide.region_5.6_spmd.clone.sunk | while | flops 73400320 | bytes 550997 | solution.py:16
  130.6 1.8 dynamic_update_slice.6
  134.8 1.8 dynamic_update_slice.6
  155.8 1.8 dynamic_update_slice.6
  160.0 1.8 dynamic_update_slice.6
  164.2 1.8 dynamic_update_slice.6
  168.5 1.8 dynamic_update_slice.6
  172.7 1.8 dynamic_update_slice.6
  193.7 1.8 dynamic_update_slice.6
  197.9 1.8 dynamic_update_slice.6
  666.6 6.3 reshape.94
  672.9 6.9 %copy.42 = f32[2,128,17,2,128]{1,2,3,4,0:T(8,128)} copy(f32[2,128,17,2,128]{4,3,1,2,0:T(2,128)} %reshape.94) | data formatting | bytes 8912896 | tf_op jit(solution)/shard_map/reshape.6
  679.8 3.2 fusion.23
  686.8 5.4 pmax.7
  (534 shorter events, 530.2 us)
Async XLA Ops:
  0.6 13.5 %copy-start.1 = (bf16[128,4096]{1,0:T(8,128)(2,1)S(1)}, bf16[128,4096]{1,0:T(8,128)(2,1)}, u32[]{:S(2)}) copy-start(bf16[128,4096]{1,0:T(8,128)(2,1)} %param.7) | copy-start | bytes 3145732
  45.9 59.8 %all-to-all-start = ((bf16[145,16,2,256]{3,2,0,1:T(2,128)(2,1)}), bf16[145,16,2,256]{3,2,0,1:T(2,128)(2,1)S(1)}, u32[]{:S(2)}, u32[]{:S(2)}) async-start(bf16[145,16,2,256]{3,2,0,1:T(2,128)(2,1)} %copy.36), calls=%async_computation | async-start | bytes 4751360 | tf_op jit(solution)/shard_map/all_to_all | solution.py:41
  114.4 2.8 copy-start
where the time goes:
time: 706 us; the launch traced here: 692 us
  local copies, waits for them, and re-layouts  396 us (56%)
  matrix products  207 us (29%)
  waiting for transfers between devices  53.6 us (8%)
  other arithmetic  21 us (3%)
    dynamic_update_slice x256, local copies, waits for them, and re-layouts, feature_histograms(): stacked = lax.map(one_feature, bin_table)  232 us
    dot_general x128, matrix products, one_feature(): jnp.einsum('skr,krb->ksb', statistics, indicator, preferred_element_type=...  207 us
    eq x128, local copies, waits for them, and re-layouts, one_feature(): indicator = (bin_row[:, :, None] == levels).astype(jnp.bfloat16)  97.3 us
    all_to_all x1, waiting for transfers between devices, on_device(): lax.all_to_all(outgoing, 'node', split_axis=1, concat_axis=3, tiled=True)  53.6 us
    scatter x1, local copies, waits for them, and re-layouts, on_device(): jnp.zeros((payload_width, node_total * capacity), jnp.bfloat16)  20.6 us
    another operation x4, local copies, waits for them, and re-layouts  14.5 us
  transfers between devices with their start and end apart: 1, of which 1 were waited for; matrix products, arithmetic and copies ran while one was open for 0% of the time, Pallas kernels for 0%

commit v1 on v0

v1 whole, which is shorter than its diff:
```python
import functools

import jax
import jax.numpy as jnp
from jax import lax
from jax.experimental import pallas as pl
from jax.experimental.pallas import tpu as pltpu
from jax.sharding import PartitionSpec as P

B = 256
HI = 4
LO = B // HI
LANES = 128
VMEM = 56 * 1024 * 1024
NT = (((1,), (1,)), ((), ()))


def triangle():
    row = lax.broadcasted_iota(jnp.int32, (B, B), 0)
    column = lax.broadcasted_iota(jnp.int32, (B, B), 1)
    return jnp.where(row <= column, 1.0, 0.0).astype(jnp.bfloat16)


def rank_kernel(honest_ref, destination_ref, slot_ref, target_ref, rank_ref, count_ref):
    nodes = slot_ref.shape[0]
    rows = honest_ref.shape[1]
    upper = triangle()
    index = lax.broadcasted_iota(jnp.int32, (nodes, B), 0)
    carry = jnp.zeros((nodes, 1), jnp.float32)
    for block in range(rows // B):
        span = pl.ds(block * B, B)
        named = destination_ref[:, span] == index
        target = jnp.sum(jnp.where(named, slot_ref[...], 0), axis=0, keepdims=True)
        active = honest_ref[:, span] == 0
        owned = jnp.where((target == index) & active, 1.0, 0.0)
        upto = jnp.dot(owned.astype(jnp.bfloat16), upper, preferred_element_type=jnp.float32) + carry
        rank = jnp.sum(owned * upto, axis=0, keepdims=True) - 1.0
        target_ref[:, span] = target.astype(jnp.float32)
        rank_ref[:, span] = rank
        carry = upto[:, B - 1 : B]
    count_ref[...] = jnp.broadcast_to(carry, count_ref.shape)


def ranks(honest, destination, node_slot):
    rows = honest.shape[0]
    nodes = node_slot.shape[0]
    return pl.pallas_call(
        rank_kernel,
        out_shape=(
            jax.ShapeDtypeStruct((1, rows), jnp.float32),
            jax.ShapeDtypeStruct((1, rows), jnp.float32),
            jax.ShapeDtypeStruct((nodes, LANES), jnp.float32),
        ),
        compiler_params=pltpu.CompilerParams(vmem_limit_bytes=VMEM),
    )(honest.reshape(1, rows), destination.reshape(1, rows), node_slot.reshape(nodes, 1))


def permute_kernel(capacity, local, parts, cov_ref, pseudo_ref, target_ref, rank_ref, *rest):
    outs, (payload, place) = rest[: parts + 1], rest[parts + 1 :]
    device = pl.program_id(0)
    features = cov_ref.shape[0]
    rows = cov_ref.shape[1]

    @pl.when(device == 0)
    def _():
        level = jnp.floor(cov_ref[...].astype(jnp.float32) * B) + 1.0
        payload[0:features, :] = level.astype(jnp.bfloat16)
        payload[features : features + 16, :] = pseudo_ref[...]

    step = 512
    for n in range(local):
        node = (device * local + n).astype(jnp.float32)
        for c in range(rows // step):
            span = pl.ds(c * step, step)
            key = jnp.where(target_ref[:, span] == node, rank_ref[:, span], -1.0)
            key = jnp.broadcast_to(key, (16, step)).astype(jnp.bfloat16)
            for j in range(capacity // 16):
                at = lax.broadcasted_iota(jnp.int32, (16, step), 0).astype(jnp.float32) + float(16 * j)
                hit = jnp.where(key == at.astype(jnp.bfloat16), jnp.bfloat16(1), jnp.bfloat16(0))
                place[n * capacity + 16 * j : n * capacity + 16 * j + 16, span] = hit
    moved = lax.dot_general(payload[...], place[...], NT, preferred_element_type=jnp.float32)
    moved = moved.astype(jnp.bfloat16)
    each = features // parts
    for k in range(parts):
        outs[k][0] = moved[k * each : (k + 1) * each]
    outs[parts][0] = moved[features:]


def permute(covariates, pseudo, target, rank, capacity, local, devices, parts):
    features, rows = covariates.shape
    width = local * capacity
    each = features // parts
    whole = lambda d: (0, 0)
    sizes = [each] * parts + [16]
    return pl.pallas_call(
        functools.partial(permute_kernel, capacity, local, parts),
        grid=(devices,),
        in_specs=[
            pl.BlockSpec((features, rows), whole),
            pl.BlockSpec((16, rows), whole),
            pl.BlockSpec((1, rows), whole),
            pl.BlockSpec((1, rows), whole),
        ],
        out_specs=[pl.BlockSpec((1, size, width), lambda d: (d, 0, 0)) for size in sizes],
        out_shape=[jax.ShapeDtypeStruct((devices, size, width), jnp.bfloat16) for size in sizes],
        scratch_shapes=[
            pltpu.VMEM((features + 16, rows), jnp.bfloat16),
            pltpu.VMEM((width, rows), jnp.bfloat16),
        ],
        compiler_params=pltpu.CompilerParams(vmem_limit_bytes=VMEM),
    )(covariates, pseudo, target, rank)


def gather_rows(arrived, node, capacity, store):
    devices = arrived.shape[0]
    head = capacity // LANES * LANES
    tail = capacity - head
    first = 0 if node == 0 else head + 2 * tail
    for s in range(devices):
        store(s * head, arrived[s, :, first : first + head].astype(jnp.float32))
    if tail:
        for i in range(devices // 2):
            one = arrived[2 * i, :, head : head + LANES].astype(jnp.float32)
            two = arrived[2 * i + 1, :, head : head + LANES].astype(jnp.float32)
            lane = lax.broadcasted_iota(jnp.int32, one.shape, 1)
            if node == 0:
                mixed = jnp.where(lane < tail, one, pltpu.roll(two, tail, 1))
            else:
                mixed = jnp.where(lane < tail, pltpu.roll(one, tail, 1), two)
            store(devices * head + i * LANES, mixed)


def histogram_kernel(capacity, local, chained, arrived, stats, *rest):
    if chained:
        rest = rest[1:]
    out_ref, best_ref, high, low, values, left_side, right_side = rest
    group = pl.program_id(0)
    rows = high.shape[2]

    @pl.when(group == 0)
    def _():
        best_ref[...] = jnp.full(best_ref.shape, -jnp.inf, jnp.float32)
        for n in range(local):

            def store(at, part):
                level = part - 1.0
                upper = jnp.floor(level * (1.0 / LO))
                span = slice(at, at + part.shape[1])
                high[n, :, span] = upper
                low[n, :, span] = level - upper * LO

            def store_values(at, part):
                values[n, :, at : at + part.shape[1]] = part.astype(jnp.bfloat16)

            gather_rows(arrived, n, capacity, store)
            gather_rows(stats, n, capacity, store_values)

    upper = triangle()
    step = 512
    sub = lax.broadcasted_iota(jnp.int32, (16, step), 0)
    subf = sub.astype(jnp.float32)
    zero, one = jnp.bfloat16(0), jnp.bfloat16(1)
    for n in range(local):
        for c in range(rows // step):
            span = pl.ds(c * step, step)
            stat = values[n, :, span]
            mixed = None
            for f in range(4):
                top = jnp.broadcast_to(high[n, pl.ds(group * 4 + f, 1), span], (16, step))
                bottom = jnp.broadcast_to(low[n, pl.ds(group * 4 + f, 1), span], (16, step)).astype(jnp.bfloat16)
                mixed = top if f == 0 else jnp.where(sub >= 4 * f, top, mixed)
                top = top.astype(jnp.bfloat16)
                for h in range(HI):
                    left_side[(f * HI + h) * 16 : (f * HI + h + 1) * 16, span] = jnp.where(top == jnp.bfloat16(h), stat, zero)
                for j in range(LO // 16):
                    at = (subf + float(16 * j)).astype(jnp.bfloat16)
                    right_side[f * LO + 16 * j : f * LO + 16 * j + 16, span] = jnp.where(bottom == at, one, zero)
            wanted = (sub % 4).astype(jnp.float32)
            left_side[256:272, span] = jnp.where(mixed == wanted, 1.0, 0.0).astype(jnp.bfloat16)
        sums = lax.dot_general(left_side[...], right_side[...], NT, preferred_element_type=jnp.float32)
        pieces = []
        weights = []
        for f in range(4):
            lanes = slice(f * LO, (f + 1) * LO)
            piece = jnp.concatenate([sums[(f * HI + h) * 16 : (f * HI + h + 1) * 16, lanes] for h in range(HI)], axis=1)
            weight = jnp.concatenate([sums[256 + f * HI + h : 257 + f * HI + h, lanes] for h in range(HI)], axis=1)
            out_ref[n, f, 0:1] = weight
            out_ref[n, f, 1:17] = piece
            pieces.append(piece)
            weights.append(weight)
        table = jnp.concatenate(pieces + weights + [jnp.zeros((4, B), jnp.float32)], axis=0)
        first = table.astype(jnp.bfloat16)
        table = table - first.astype(jnp.float32)
        second = table.astype(jnp.bfloat16)
        third = (table - second.astype(jnp.float32)).astype(jnp.bfloat16)
        left = (
            jnp.dot(third, upper, preferred_element_type=jnp.float32)
            + jnp.dot(second, upper, preferred_element_type=jnp.float32)
            + jnp.dot(first, upper, preferred_element_type=jnp.float32)
        )
        total = left[:, B - 1 : B]
        right = total - left
        for f in range(4):
            span = slice(16 * f, 16 * f + 16)
            count = slice(64 + f, 65 + f)
            squared = lambda side: jnp.sum(side[span] * side[span], axis=0, keepdims=True) / (side[count] + 1.0)
            gain = squared(left) + squared(right) - squared(total)
            best_ref[n : n + 1, :] = jnp.maximum(best_ref[n : n + 1, :], gain)


def histogram_part(arrived, stats, previous, part, features, capacity, local):
    devices, each, width = arrived.shape
    rows = devices * capacity
    groups = each // 4
    whole = lambda g: (0, 0, 0)
    in_specs = [pl.BlockSpec((devices, each, width), whole), pl.BlockSpec((devices, 16, width), whole)]
    operands = [arrived, stats]
    chained = previous is not None
    if chained:
        in_specs.append(pl.BlockSpec(memory_space=pl.ANY))
        operands.append(previous)
    return pl.pallas_call(
        functools.partial(histogram_kernel, capacity, local, chained),
        grid=(groups,),
        in_specs=in_specs,
        out_specs=[
            pl.BlockSpec((local, 4, 17, B), lambda g: (0, part * groups + g, 0, 0)),
            pl.BlockSpec((local, B), lambda g: (0, 0)),
        ],
        out_shape=[
            jax.ShapeDtypeStruct((local, features, 17, B), jnp.float32),
            jax.ShapeDtypeStruct((local, B), jnp.float32),
        ],
        scratch_shapes=[
            pltpu.VMEM((local, each, rows), jnp.float32),
            pltpu.VMEM((local, each, rows), jnp.float32),
            pltpu.VMEM((local, 16, rows), jnp.bfloat16),
            pltpu.VMEM((272, rows), jnp.bfloat16),
            pltpu.VMEM((256, rows), jnp.bfloat16),
        ],
        input_output_aliases={2: 0} if chained else {},
        compiler_params=pltpu.CompilerParams(vmem_limit_bytes=VMEM),
        cost_estimate=pl.CostEstimate(
            flops=2 * local * groups * 272 * 256 * rows, bytes_accessed=arrived.size * 2, transcendentals=0
        ),
    )(*operands)


def finish(sent, features, capacity, local):
    parts = len(sent) - 1
    swap = lambda block: lax.all_to_all(block, "node", split_axis=0, concat_axis=0, tiled=True)
    stats = swap(sent[parts])
    arrived = [swap(block) for block in sent[:parts]]
    histogram, best = None, None
    for k in range(parts):
        histogram, part_best = histogram_part(arrived[k], stats, histogram, k, features, capacity, local)
        best = part_best if best is None else jnp.maximum(best, part_best)
    return histogram, best


def on_device(covariates, pseudo, honest, destination, node_slot):
    features, rows = covariates.shape
    devices = lax.axis_size("node")
    nodes = node_slot.shape[0]
    local = nodes // devices
    most = 2 * rows // nodes
    parts = max(1, min(4, features // 16))
    small = most - 64 if most % LANES == 0 and most > LANES else most
    target, rank, count = ranks(honest, destination, node_slot)

    def route(capacity):
        return permute(covariates, pseudo, target, rank, capacity, local, devices, parts)

    if small < most:
        over = lax.pmax(jnp.max(count), "node") > small
        quick = route(small)
        histogram, best = lax.cond(
            over,
            lambda: tuple(finish(route(most), features, most, local)),
            lambda: tuple(finish(quick, features, small, local)),
        )
    else:
        histogram, best = finish(route(most), features, most, local)
    best_gain = lax.pmax(jnp.max(best, axis=1), "feat")
    return (histogram, best_gain)


def solution(mesh):
    placed = (P("feat", "node"), P(None, "node"), P("node"), P("node", None), P())
    return jax.shard_map(
        on_device,
        mesh=mesh,
        in_specs=placed,
        out_specs=(P("node", "feat", None, None), P("node")),
        check_vma=False,
    )
```

time: 706 us -> 234 us (0.33); the launches traced: 692 us -> 232 us
  local copies, waits for them, and re-layouts: 396 us -> 24.7 us
  matrix products: 207 us -> 0 us
  Pallas kernels: 0 us -> 112 us
  blocking collectives: 5.43 us -> 81.9 us
  waiting for transfers between devices: 53.6 us -> 0.01 us
  other arithmetic: 21 us -> 1.44 us
    dynamic_update_slice x256 -> x0, local copies, waits for them, and re-layouts: 232 us -> none  [feature_histograms(): stacked = lax.map(one_feature, bin_table)]
    dot_general x128 -> x0, matrix products: 207 us -> none  [one_feature(): jnp.einsum('skr,krb->ksb', statistics, indicator, preferred_element_type=...]
    pallas_call x0 -> x6, Pallas kernels: none -> 112 us  [the longest x4 89.3 us: histogram_part(): pl.pallas_call(functools.partial(histogram_kernel, capacity, local, chain...]
    eq x128 -> x0, local copies, waits for them, and re-layouts: 97.3 us -> none  [one_feature(): indicator = (bin_row[:, :, None] == levels).astype(jnp.bfloat16)]
    all_to_all x1 -> x2, waiting for transfers between devices: 53.6 us -> 0.01 us  [finish(): lax.all_to_all(block, 'node', split_axis=0, concat_axis=0, tiled=True)]
    all_to_all x0 -> x3, blocking collectives: none -> 52.7 us  [finish(): lax.all_to_all(block, 'node', split_axis=0, concat_axis=0, tiled=True)]
    pmax x1 -> x2, blocking collectives: 5.43 us -> 29.2 us  [the longest x1 23.7 us: on_device(): over = lax.pmax(jnp.max(count), 'node') > small]
    scatter x1 -> x0, local copies, waits for them, and re-layouts: 20.6 us -> none  [on_device(): jnp.zeros((payload_width, node_total * capacity), jnp.bfloat16)]
  transfers between devices with their start and end apart: 1 -> 2, of which waited for: 1 -> 0; matrix products, arithmetic and copies ran while one was open for 0% -> 5% of each run, Pallas kernels for 0% -> 29%
where the time goes in v1:
time: 234 us; the launch traced here: 232 us
  Pallas kernels  112 us (48%)
  blocking collectives  81.9 us (35%)
  local copies, waits for them, and re-layouts  24.7 us (11%)
  starting transfers between devices  10.7 us (5%)
    pallas_call x4, Pallas kernels, histogram_part(): pl.pallas_call(functools.partial(histogram_kernel, capacity, local, chain...  89.3 us
    all_to_all x3, blocking collectives, finish(): lax.all_to_all(block, 'node', split_axis=0, concat_axis=0, tiled=True)  52.7 us
    pmax x1, blocking collectives, on_device(): over = lax.pmax(jnp.max(count), 'node') > small  23.7 us
    pallas_call x1, Pallas kernels, permute(): pl.pallas_call(functools.partial(permute_kernel, capacity, local, parts),...  20.3 us
    cond x13, local copies, waits for them, and re-layouts  17.2 us
    all_to_all x2, starting transfers between devices, finish(): lax.all_to_all(block, 'node', split_axis=0, concat_axis=0, tiled=True)  10.7 us
    unnamed x1, local copies, waits for them, and re-layouts  6.21 us
    pmax x1, blocking collectives, on_device(): best_gain = lax.pmax(jnp.max(best, axis=1), 'feat')  5.44 us
  transfers between devices with their start and end apart: 2, of which 0 were waited for; matrix products, arithmetic and copies ran while one was open for 5% of the time, Pallas kernels for 29%

profile of v1, /device:TPU:20, one launch (start us, length us, event | category | flops | bytes accessed | tf_op | source)
XLA Modules:
  0.0 232.4 jit_solution(5254868137335803010)
XLA Ops:
  0.6 1.3 copy.13.slot_ref
  2.0 2.7 %shard_map.68 = (f32[1,4096]{1,0:T(1,128)S(1)}, f32[1,4096]{1,0:T(1,128)S(1)}, f32[32,128]{1,0:T(8,128)}) custom-call(s32[1,4096]{1,0:T(1,128)} %bitcast.3, s32[1,4096]{1,0:T(1,128)} %bitcast.4, s32[32,1]{1,0:T(8,128)} %copy.13.slot_ref), custom_call_target="tpu_custom_call" | custom-call | tf_op jit(solution)/shard_map/pallas_call | solution.py:47
  4.6 1.3 reduce_max.18
  6.0 23.7 %pmax.14 = f32[]{:T(128)} all-reduce(f32[]{:T(128)} %reduce_max.18), channel_id=1, replica_groups=mesh['node'=16,'feat'=2] {'node'}, use_global_device_ids=true, to_apply=%region_1.0 | all-reduce | flops 1 | bytes 8 | tf_op jit(solution)/shard_map/pmax | solution.py:275
  30.3 20.3 %shard_map.69 = (bf16[16,32,384]{2,1,0:T(8,128)(2,1)S(1)}, bf16[16,32,384]{2,1,0:T(8,128)(2,1)}, bf16[16,32,384]{2,1,0:T(8,128)(2,1)S(1)}, bf16[16,32,384]{2,1,0:T(8,128)(2,1)}, bf16[16,16,384]{2,1,0:T(8,128)(2,1)S(1)}) custom-call(bf16[128,4096]{1,0:T(8,128)(2,1)} %cov_ref.1, bf16[16,4096]{1,0:T(8,128)(2,1)} %pseudo_ref.1, ...), custom_call_target="tpu_custom_call" | custom-call | tf_op jit(solution)/shard_map/pallas_call | solution.py:95
  50.6 170.0 %conditional.1 = (f32[2,128,17,256]{3,2,1,0:T(8,128)}, f32[2,256]{1,0:T(2,128)S(1)}, f32[2,128,17,256]{3,2,1,0:T(8,128)}, f32[2,256]{1,0:T(2,128)S(1)}, f32[2,12...) conditional(s32[]{:T(128)} %convert_element_type.3, ...), branch_computations={%region_2.0_spmd, %region_3.0_spmd} | conditional | flops 36507222016 | bytes 92274960 | solution.py:277
  50.6 20.7 %all_to_all.40.stats = bf16[16,16,384]{2,1,0:T(8,128)(2,1)} all-to-all(bf16[16,16,384]{2,1,0:T(8,128)(2,1)S(1)} %get-tuple-element.23), channel_id=1, replica_groups=mesh['node'=16,'feat'=2] {'node'}, dimensions={0} | all-to-all | bytes 393216 | tf_op jit(solution)/shard_map/cond/branch_0_fun/all_to_all | solution.py:251
  71.3 16.5 %all_to_all.41.arrived = bf16[16,32,384]{2,1,0:T(8,128)(2,1)} all-to-all(bf16[16,32,384]{2,1,0:T(8,128)(2,1)S(1)} %get-tuple-element.24), channel_id=1, replica_groups=mesh['node'=16,'feat'=2] {'node'}, dimensions={0} | all-to-all | bytes 786432 | tf_op jit(solution)/shard_map/cond/branch_0_fun/all_to_all | solution.py:251
  87.8 15.6 %all_to_all.42.arrived = bf16[16,32,384]{2,1,0:T(8,128)(2,1)} all-to-all(bf16[16,32,384]{2,1,0:T(8,128)(2,1)S(1)} %get-tuple-element.26), channel_id=1, replica_groups=mesh['node'=16,'feat'=2] {'node'}, dimensions={0} | all-to-all | bytes 786432 | tf_op jit(solution)/shard_map/cond/branch_0_fun/all_to_all | solution.py:251
  103.4 4.6 %all-to-all-start.3 = ((bf16[16,32,384]{2,1,0:T(8,128)(2,1)}), bf16[16,32,384]{2,1,0:T(8,128)(2,1)S(1)}, u32[]{:S(2)}, u32[]{:S(2)}) async-start(bf16[16,32,384]{2,1,0:T(8,128)(2,1)} %get-tuple-element.25), calls=%async_computation.3 | async-start | bytes 786432 | tf_op jit(solution)/shard_map/cond/branch_0_fun/all_to_all | solution.py:251
  108.0 22.0 %branch_0_fun.4 = (f32[2,128,17,256]{3,2,1,0:T(8,128)S(1)}, f32[2,256]{1,0:T(2,128)S(1)}) custom-call(bf16[16,32,384]{2,1,0:T(8,128)(2,1)} %all_to_all.42.arrived, bf16[16,16,384]{2,1,0:T(8,128)(2,1)} %all_to_all.40.stats), custom_call_target="tpu_custom_call" | custom-call | flops 6845104128 | bytes 393216 | tf_op jit(solution)/shard_map/cond/branch_0_fun/pallas_call | solution.py:222
  130.0 2.6 %copy-done = f32[2,128,17,256]{3,2,1,0:T(8,128)} copy-done((f32[2,128,17,256]{3,2,1,0:T(8,128)}, f32[2,128,17,256]{3,2,1,0:T(8,128)S(1)}, u32[]{:S(2)}) %copy-start) | copy-done | bytes 4456472 | tf_op jit(solution)/shard_map/cond
  132.6 2.7 %copy.25 = f32[2,128,17,256]{3,2,1,0:T(8,128)} copy(f32[2,128,17,256]{3,2,1,0:T(8,128)S(1)} %get-tuple-element.86.rest_0_) | data formatting | bytes 8912896 | tf_op jit(solution)/shard_map/cond
  135.3 6.0 %all-to-all-start = ((bf16[16,32,384]{2,1,0:T(8,128)(2,1)}), bf16[16,32,384]{2,1,0:T(8,128)(2,1)S(1)}, u32[]{:S(2)}, u32[]{:S(2)}) async-start(bf16[16,32,384]{2,1,0:T(8,128)(2,1)} %get-tuple-element.22), calls=%async_computation | async-start | bytes 786432 | tf_op jit(solution)/shard_map/cond/branch_0_fun/all_to_all | solution.py:251
  141.3 22.7 %branch_0_fun.5 = (f32[2,128,17,256]{3,2,1,0:T(8,128)}, f32[2,256]{1,0:T(2,128)S(1)}) custom-call(bf16[16,32,384]{2,1,0:T(8,128)(2,1)} %copy-done.9, bf16[16,16,384]{2,1,0:T(8,128)(2,1)} %all_to_all.40.stats, f32[2,128,17,256]{3,2,1,0:T(8,128)} %copy-done), custom_call_target="tpu_custom_call", output_to_operand_aliasing={{0}: (2, {})} | custom-call | flops 6845104128 | bytes 393216 | tf_op jit(solution)/shard_map/cond/branch_0_fun/pallas_call | solution.py:222
  164.0 6.0 %copy.27 = f32[2,128,17,256]{3,2,1,0:T(8,128)} copy(f32[2,128,17,256]{3,2,1,0:T(8,128)} %get-tuple-element.88.rest_0_) | data formatting | bytes 8912896 | tf_op jit(solution)/shard_map/cond
  170.0 22.0 %branch_0_fun.6 = (f32[2,128,17,256]{3,2,1,0:T(8,128)S(1)}, f32[2,256]{1,0:T(2,128)S(1)}) custom-call(bf16[16,32,384]{2,1,0:T(8,128)(2,1)} %all_to_all.41.arrived, bf16[16,16,384]{2,1,0:T(8,128)(2,1)} %all_to_all.40.stats, f32[2,128,17,256]{3,2,1,0:T(8,128)S(1)} %copy-done.1), custom_call_target="tpu_custom_call", output_to_operand_aliasing={{0}: (2, {})} | custom-call | flops 6845104128 | bytes 393216 | tf_op jit(solution)/shard_map/cond/branch_0_fun/pallas_call | solution.py:222
  192.0 2.6 %copy-done.2 = f32[2,128,17,256]{3,2,1,0:T(8,128)} copy-done((f32[2,128,17,256]{3,2,1,0:T(8,128)}, f32[2,128,17,256]{3,2,1,0:T(8,128)S(1)}, u32[]{:S(2)}) %copy-start.2) | copy-done | bytes 4456472 | tf_op jit(solution)/shard_map/cond
  194.6 2.6 %copy.23 = f32[2,128,17,256]{3,2,1,0:T(8,128)} copy(f32[2,128,17,256]{3,2,1,0:T(8,128)S(1)} %get-tuple-element.84.rest_0_) | data formatting | bytes 8912896 | tf_op jit(solution)/shard_map/cond
  197.2 0.7 copy-done.8
  197.9 22.7 %branch_0_fun.7 = (f32[2,128,17,256]{3,2,1,0:T(8,128)}, f32[2,256]{1,0:T(2,128)S(1)}) custom-call(bf16[16,32,384]{2,1,0:T(8,128)(2,1)} %copy-done.8, bf16[16,16,384]{2,1,0:T(8,128)(2,1)} %all_to_all.40.stats, f32[2,128,17,256]{3,2,1,0:T(8,128)} %copy-done.2), custom_call_target="tpu_custom_call", output_to_operand_aliasing={{0}: (2, {})} | custom-call | flops 6845104128 | bytes 393216 | tf_op jit(solution)/shard_map/cond/branch_0_fun/pallas_call | solution.py:222
  220.6 6.2 %copy.14 = f32[2,128,17,256]{3,1,2,0:T(8,128)} copy(f32[2,128,17,256]{3,2,1,0:T(8,128)} %get-tuple-element.80) | data formatting | bytes 8912896
  226.8 0.1 maximum_reduce_fusion
  226.9 5.4 %pmax.15 = f32[2]{0:T(128)} all-reduce(f32[2]{0:T(128)S(1)} %maximum_reduce_fusion), channel_id=1, replica_groups=mesh['node'=16,'feat'=2] {'feat'}, use_global_device_ids=true, to_apply=%region_5.0 | all-reduce | flops 2 | bytes 16 | tf_op jit(solution)/shard_map/pmax | solution.py:284
  (9 shorter events, 0.0 us)
Async XLA Ops:
  103.4 31.9 %all-to-all-start.3 = ((bf16[16,32,384]{2,1,0:T(8,128)(2,1)}), bf16[16,32,384]{2,1,0:T(8,128)(2,1)S(1)}, u32[]{:S(2)}, u32[]{:S(2)}) async-start(bf16[16,32,384]{2,1,0:T(8,128)(2,1)} %get-tuple-element.25), calls=%async_computation.3 | async-start | bytes 786432 | tf_op jit(solution)/shard_map/cond/branch_0_fun/all_to_all | solution.py:251
  130.0 2.6 %copy-start = (f32[2,128,17,256]{3,2,1,0:T(8,128)}, f32[2,128,17,256]{3,2,1,0:T(8,128)S(1)}, u32[]{:S(2)}) copy-start(f32[2,128,17,256]{3,2,1,0:T(8,128)S(1)} %get-tuple-element.86.rest_0_) | copy-start | bytes 13369348 | tf_op jit(solution)/shard_map/cond
  135.3 6.0 %copy-start.9 = (bf16[16,32,384]{2,1,0:T(8,128)(2,1)}, bf16[16,32,384]{2,1,0:T(8,128)(2,1)S(1)}, u32[]{:S(2)}) copy-start(bf16[16,32,384]{2,1,0:T(8,128)(2,1)S(1)} %all-to-all-done.3.arrived) | copy-start | bytes 1179652 | tf_op jit(solution)/shard_map/cond
  135.3 61.9 %all-to-all-start = ((bf16[16,32,384]{2,1,0:T(8,128)(2,1)}), bf16[16,32,384]{2,1,0:T(8,128)(2,1)S(1)}, u32[]{:S(2)}, u32[]{:S(2)}) async-start(bf16[16,32,384]{2,1,0:T(8,128)(2,1)} %get-tuple-element.22), calls=%async_computation | async-start | bytes 786432 | tf_op jit(solution)/shard_map/cond/branch_0_fun/all_to_all | solution.py:251
  164.0 6.0 %copy-start.1 = (f32[2,128,17,256]{3,2,1,0:T(8,128)S(1)}, f32[2,128,17,256]{3,2,1,0:T(8,128)}, u32[]{:S(2)}) copy-start(f32[2,128,17,256]{3,2,1,0:T(8,128)} %get-tuple-element.88.rest_0_) | copy-start | bytes 13369348 | tf_op jit(solution)/shard_map/cond
  192.0 2.6 %copy-start.2 = (f32[2,128,17,256]{3,2,1,0:T(8,128)}, f32[2,128,17,256]{3,2,1,0:T(8,128)S(1)}, u32[]{:S(2)}) copy-start(f32[2,128,17,256]{3,2,1,0:T(8,128)S(1)} %get-tuple-element.84.rest_0_) | copy-start | bytes 13369348 | tf_op jit(solution)/shard_map/cond
  197.2 0.7 copy-start.8

commit v2 on v1

v2 whole, which is shorter than its diff:
```python
import functools
import math

import jax
import jax.numpy as jnp
from jax import lax
from jax.experimental import pallas as pl
from jax.experimental.pallas import tpu as pltpu
from jax.sharding import PartitionSpec as P

B = 256
HI = 4
LO = B // HI
LANES = 128
POISON = 512.0
VMEM = 48 * 1024 * 1024
NT = (((1,), (1,)), ((), ()))


def triangle():
    row = lax.broadcasted_iota(jnp.int32, (B, B), 0)
    column = lax.broadcasted_iota(jnp.int32, (B, B), 1)
    return jnp.where(row <= column, 1.0, 0.0).astype(jnp.bfloat16)


def rank_kernel(honest_ref, destination_ref, slot_ref, target_ref, rank_ref, count_ref):
    nodes = slot_ref.shape[0]
    rows = honest_ref.shape[1]
    upper = triangle()
    index = lax.broadcasted_iota(jnp.int32, (nodes, B), 0)
    carry = jnp.zeros((nodes, 1), jnp.float32)
    for block in range(rows // B):
        span = pl.ds(block * B, B)
        named = destination_ref[:, span] == index
        target = jnp.sum(jnp.where(named, slot_ref[...], 0), axis=0, keepdims=True)
        active = honest_ref[:, span] == 0
        owned = jnp.where((target == index) & active, 1.0, 0.0)
        upto = jnp.dot(owned.astype(jnp.bfloat16), upper, preferred_element_type=jnp.float32) + carry
        rank = jnp.sum(owned * upto, axis=0, keepdims=True) - 1.0
        target_ref[:, span] = target.astype(jnp.float32)
        rank_ref[:, span] = rank
        carry = upto[:, B - 1 : B]
    count_ref[...] = jnp.broadcast_to(carry, count_ref.shape)


def ranks(honest, destination, node_slot):
    rows = honest.shape[0]
    nodes = node_slot.shape[0]
    return pl.pallas_call(
        rank_kernel,
        out_shape=(
            jax.ShapeDtypeStruct((1, rows), jnp.float32),
            jax.ShapeDtypeStruct((1, rows), jnp.float32),
            jax.ShapeDtypeStruct((nodes, LANES), jnp.float32),
        ),
        compiler_params=pltpu.CompilerParams(vmem_limit_bytes=VMEM),
    )(honest.reshape(1, rows), destination.reshape(1, rows), node_slot.reshape(nodes, 1))


def permute_kernel(capacity, local, pair, cov_ref, pseudo_ref, target_ref, rank_ref, count_ref, *rest):
    outs, payload, places = rest[: -1 - pair * local], rest[-1 - pair * local], rest[-pair * local :]
    group = pl.program_id(0)
    rows = cov_ref.shape[1]
    head = capacity // LANES * LANES
    tail = capacity - head

    @pl.when(group == 0)
    def _():
        payload[0:16, :] = pseudo_ref[...]
        level = jnp.floor(cov_ref[...].astype(jnp.float32) * B) + 1.0
        payload[16:, :] = level.astype(jnp.bfloat16)

    over = jnp.max(count_ref[...], axis=0, keepdims=True)[:, 0:1] > float(capacity)
    step = math.gcd(rows, 512)
    for d in range(pair):
        for n in range(local):
            place = places[d * local + n]
            node = ((group * pair + d) * local + n).astype(jnp.float32)
            for c in range(rows // step):
                span = pl.ds(c * step, step)
                key = jnp.where(target_ref[:, span] == node, rank_ref[:, span], -1.0)
                key = jnp.broadcast_to(key, (16, step)).astype(jnp.bfloat16)
                for j in range(capacity // 16):
                    at = lax.broadcasted_iota(jnp.int32, (16, step), 0).astype(jnp.float32) + float(16 * j)
                    hit = jnp.where(key == at.astype(jnp.bfloat16), jnp.bfloat16(1), jnp.bfloat16(0))
                    place[16 * j : 16 * j + 16, span] = hit
            moved = lax.dot_general(payload[...], place[...], NT, preferred_element_type=jnp.float32)
            first = 0
            for out in outs:
                size = out.shape[1]
                part = moved[first : first + size]
                if first == 0:
                    part = jnp.where(over, POISON, part)
                part = part.astype(jnp.bfloat16)
                out[d, :, n * head : (n + 1) * head] = part[:, :head]
                if tail:
                    at = local * head + n * tail
                    out[d, :, at : at + tail] = part[:, head:]
                first += size


def permute(covariates, pseudo, target, rank, count, capacity, local, devices, sizes):
    features, rows = covariates.shape
    width = local * capacity
    pair = 2 if devices % 2 == 0 else 1
    whole = lambda d: (0, 0)
    return pl.pallas_call(
        functools.partial(permute_kernel, capacity, local, pair),
        grid=(devices // pair,),
        in_specs=[
            pl.BlockSpec((features, rows), whole),
            pl.BlockSpec((16, rows), whole),
            pl.BlockSpec((1, rows), whole),
            pl.BlockSpec((1, rows), whole),
            pl.BlockSpec(count.shape, whole),
        ],
        out_specs=[pl.BlockSpec((pair, size, width), lambda d: (d, 0, 0)) for size in sizes],
        out_shape=[jax.ShapeDtypeStruct((devices, size, width), jnp.bfloat16) for size in sizes],
        scratch_shapes=[pltpu.VMEM((features + 16, rows), jnp.bfloat16)]
        + [pltpu.VMEM((capacity, rows), jnp.bfloat16)] * (pair * local),
        compiler_params=pltpu.CompilerParams(vmem_limit_bytes=VMEM),
    )(covariates, pseudo, target, rank, count)


def gather_rows(arrived, first, size, node, capacity, local, store):
    devices = arrived.shape[0]
    head = capacity // LANES * LANES
    tail = capacity - head
    span = slice(first, first + size)
    for s in range(devices):
        store(s * head, arrived[s, span, node * head : (node + 1) * head].astype(jnp.float32))
    if tail:
        each = LANES // tail
        lane = lax.broadcasted_iota(jnp.int32, (size, local * tail), 1)
        for i in range(devices // each):
            columns = []
            for j in range(each):
                block = arrived[each * i + j, span, local * head : local * capacity].astype(jnp.float32)
                columns.append(block[:, node * tail : (node + 1) * tail])
            store(devices * head + i * LANES, jnp.concatenate(columns, axis=1))


def histogram_kernel(capacity, local, first, size, chained, *refs):
    if chained:
        arrived, stats, _, before_ref, out_ref, best_ref, high, low, values = refs[:9]
        sides = refs[9:]
    else:
        arrived, out_ref, best_ref, high, low, values = refs[:6]
        stats = arrived
        sides = refs[6:]
    group = pl.program_id(0)
    rows = high.shape[2]

    @pl.when(group == 0)
    def _():
        if chained:
            best_ref[...] = before_ref[...]
        else:
            best_ref[...] = jnp.full(best_ref.shape, -jnp.inf, jnp.float32)
        for n in range(local):

            def store(at, part):
                level = part - 1.0
                upper = jnp.floor(level * (1.0 / LO))
                span = slice(at, at + part.shape[1])
                high[n, :, span] = upper
                low[n, :, span] = level - upper * LO

            def store_values(at, part):
                values[n, :, at : at + part.shape[1]] = part.astype(jnp.bfloat16)

            gather_rows(arrived, first, size, n, capacity, local, store)
            gather_rows(stats, 0, 16, n, capacity, local, store_values)

    upper = triangle()
    step = math.gcd(rows, 512)
    sub = lax.broadcasted_iota(jnp.int32, (16, step), 0)
    subf = sub.astype(jnp.float32)
    wanted = (sub % 4).astype(jnp.float32)
    zero, one = jnp.bfloat16(0), jnp.bfloat16(1)
    for turn in range(2 * local):
        q, n = turn // local, turn % local
        left_side, right_side = sides[2 * turn], sides[2 * turn + 1]
        for c in range(rows // step):
            span = pl.ds(c * step, step)
            stat = values[n, :, span]
            mixed = None
            for f in range(4):
                row = pl.ds(group * 8 + q * 4 + f, 1)
                top = jnp.broadcast_to(high[n, row, span], (16, step))
                bottom = jnp.broadcast_to(low[n, row, span], (16, step)).astype(jnp.bfloat16)
                mixed = top if f == 0 else jnp.where(sub >= 4 * f, top, mixed)
                top = top.astype(jnp.bfloat16)
                for h in range(HI):
                    at = (f * HI + h) * 16
                    left_side[at : at + 16, span] = jnp.where(top == jnp.bfloat16(h), stat, zero)
                for j in range(LO // 16):
                    at = (subf + float(16 * j)).astype(jnp.bfloat16)
                    right_side[f * LO + 16 * j : f * LO + 16 * j + 16, span] = jnp.where(bottom == at, one, zero)
            left_side[256:272, span] = jnp.where(mixed == wanted, 1.0, 0.0).astype(jnp.bfloat16)
        sums = lax.dot_general(left_side[...], right_side[...], NT, preferred_element_type=jnp.float32)
        pieces = []
        weights = []
        for f in range(4):
            lanes = slice(f * LO, (f + 1) * LO)
            piece = jnp.concatenate([sums[(f * HI + h) * 16 : (f * HI + h + 1) * 16, lanes] for h in range(HI)], axis=1)
            weight = jnp.concatenate([sums[256 + f * HI + h : 257 + f * HI + h, lanes] for h in range(HI)], axis=1)
            out_ref[n, 0, q * 4 + f : q * 4 + f + 1, :] = weight
            out_ref[n, 1:17, q * 4 + f, :] = piece
            pieces.append(piece)
            weights.append(weight)
        table = jnp.concatenate(pieces + weights + [jnp.zeros((4, B), jnp.float32)], axis=0)
        one_part = table.astype(jnp.bfloat16)
        table = table - one_part.astype(jnp.float32)
        two_part = table.astype(jnp.bfloat16)
        three_part = (table - two_part.astype(jnp.float32)).astype(jnp.bfloat16)
        left = (
            jnp.dot(three_part, upper, preferred_element_type=jnp.float32)
            + jnp.dot(two_part, upper, preferred_element_type=jnp.float32)
            + jnp.dot(one_part, upper, preferred_element_type=jnp.float32)
        )
        total = left[:, B - 1 : B]
        right = total - left
        for f in range(4):
            span = slice(16 * f, 16 * f + 16)
            count = slice(64 + f, 65 + f)
            squared = lambda side: jnp.sum(side[span] * side[span], axis=0, keepdims=True) / (side[count] + 1.0)
            gain = squared(left) + squared(right) - squared(total)
            best_ref[n : n + 1, :] = jnp.maximum(best_ref[n : n + 1, :], gain)


def histogram_part(arrived, stats, previous, first, size, offset, features, capacity, local):
    devices, height, width = arrived.shape
    rows = devices * capacity
    groups = size // 8
    whole = lambda g: (0, 0, 0)
    chained = previous is not None
    in_specs = [pl.BlockSpec((devices, height, width), whole)]
    operands = [arrived]
    if chained:
        in_specs += [
            pl.BlockSpec((devices, 16, width), whole),
            pl.BlockSpec(memory_space=pl.ANY),
            pl.BlockSpec((local, B), lambda g: (0, 0)),
        ]
        operands += [stats, previous[0], previous[1]]
    return pl.pallas_call(
        functools.partial(histogram_kernel, capacity, local, first, size, chained),
        grid=(groups,),
        in_specs=in_specs,
        out_specs=[
            pl.BlockSpec((local, 17, 8, B), lambda g: (0, 0, offset // 8 + g, 0)),
            pl.BlockSpec((local, B), lambda g: (0, 0)),
        ],
        out_shape=[
            jax.ShapeDtypeStruct((local, 17, features, B), jnp.float32),
            jax.ShapeDtypeStruct((local, B), jnp.float32),
        ],
        scratch_shapes=[
            pltpu.VMEM((local, size, rows), jnp.float32),
            pltpu.VMEM((local, size, rows), jnp.float32),
            pltpu.VMEM((local, 16, rows), jnp.bfloat16),
        ]
        + [pltpu.VMEM((272, rows), jnp.bfloat16), pltpu.VMEM((256, rows), jnp.bfloat16)] * (2 * local),
        input_output_aliases={2: 0} if chained else {},
        compiler_params=pltpu.CompilerParams(vmem_limit_bytes=VMEM),
        cost_estimate=pl.CostEstimate(
            flops=4 * local * groups * 272 * 256 * rows, bytes_accessed=arrived.size * 2, transcendentals=0
        ),
    )(*operands)


def swap(block):
    return lax.all_to_all(block, "node", split_axis=0, concat_axis=0, tiled=True)


def finish(first_arrived, sent, features, capacity, local):
    size = first_arrived.shape[1] - 16
    result = histogram_part(first_arrived, None, None, 16, size, 0, features, capacity, local)
    for block in sent:
        arrived = swap(block)
        result = histogram_part(
            arrived, first_arrived, result, 0, block.shape[1], size, features, capacity, local
        )
        size += block.shape[1]
    return tuple(result)


def on_device(covariates, pseudo, honest, destination, node_slot):
    features, rows = covariates.shape
    devices = lax.axis_size("node")
    nodes = node_slot.shape[0]
    local = nodes // devices
    most = 2 * rows // nodes
    early = features // 8 * 3
    early = early if early % 16 == 0 else features
    sizes = [16 + early] + ([features - early] if early < features else [])
    small = most - 96 if most % LANES == 0 and most > LANES else most
    target, rank, count = ranks(honest, destination, node_slot)

    def route(capacity):
        return permute(covariates, pseudo, target, rank, count, capacity, local, devices, sizes)

    def full():
        sent = route(most)
        return finish(swap(sent[0]), sent[1:], features, most, local)

    if small < most:
        sent = route(small)
        arrived = swap(sent[0])
        over = jnp.max(arrived[:, 0, 0]) > POISON / 2
        histogram, best = lax.cond(over, full, lambda: finish(arrived, sent[1:], features, small, local))
    else:
        histogram, best = full()
    best_gain = lax.pmax(jnp.max(best, axis=1), "feat")
    return (jnp.transpose(histogram, (0, 2, 1, 3)), best_gain)


def solution(mesh):
    placed = (P("feat", "node"), P(None, "node"), P("node"), P("node", None), P())
    return jax.shard_map(
        on_device,
        mesh=mesh,
        in_specs=placed,
        out_specs=(P("node", "feat", None, None), P("node")),
        check_vma=False,
    )
```

time: 234 us -> 124 us (0.53)
  blocking collectives: 81.9 us -> 5.44 us
  Pallas kernels: 112 us -> 82.3 us
  local copies, waits for them, and re-layouts: 24.7 us -> 2.17 us
  waiting for transfers between devices: 0.01 us -> 19.6 us
    all_to_all x3 -> x0, blocking collectives: 52.7 us -> none  [finish(): lax.all_to_all(block, 'node', split_axis=0, concat_axis=0, tiled=True)]
    pallas_call x5 -> x3, Pallas kernels: 110 us -> 81 us  [the longest x2 65.9 us: histogram_part(): pl.pallas_call(functools.partial(histogram_kernel, capacity, local, first...]
    pmax x1 -> x0, blocking collectives: 23.7 us -> none  [on_device(): over = lax.pmax(jnp.max(count), 'node') > small]
    all_to_all x2, waiting for transfers between devices: 0.01 us -> 19.6 us  [swap(): lax.all_to_all(block, 'node', split_axis=0, concat_axis=0, tiled=True)]
    cond x13 -> x0, local copies, waits for them, and re-layouts: 17.2 us -> none
    unnamed x1 -> x4, local copies, waits for them, and re-layouts: 6.21 us -> 1.43 us
  transfers between devices with their start and end apart: 2 -> 2, of which waited for: 0 -> 1; matrix products, arithmetic and copies ran while one was open for 5% -> 0% of each run, Pallas kernels for 29% -> 20%
where the time goes in v2:
time: 124 us; the launch traced here: 122 us
  Pallas kernels  82.3 us (66%)
  waiting for transfers between devices  19.6 us (16%)
  starting transfers between devices  10.8 us (9%)
  blocking collectives  5.44 us (4%)
  local copies, waits for them, and re-layouts  2.17 us (2%)
  between operations  1.29 us (1%)
    pallas_call x2, Pallas kernels, histogram_part(): pl.pallas_call(functools.partial(histogram_kernel, capacity, local, first...  65.9 us
    all_to_all x2, waiting for transfers between devices, swap(): lax.all_to_all(block, 'node', split_axis=0, concat_axis=0, tiled=True)  19.6 us
    pallas_call x1, Pallas kernels, permute(): pl.pallas_call(functools.partial(permute_kernel, capacity, local, pair),...  15.1 us
    all_to_all x2, starting transfers between devices, swap(): lax.all_to_all(block, 'node', split_axis=0, concat_axis=0, tiled=True)  10.8 us
    pmax x1, blocking collectives, on_device(): best_gain = lax.pmax(jnp.max(best, axis=1), 'feat')  5.44 us
  transfers between devices with their start and end apart: 2, of which 1 were waited for; matrix products, arithmetic and copies ran while one was open for 0% of the time, Pallas kernels for 20%

profile of v2, /device:TPU:20, one launch (start us, length us, event | category | flops | bytes accessed | tf_op | source)
XLA Modules:
  0.0 122.3 jit_solution(5944755349527158517)
XLA Ops:
  0.6 0.7 copy.9.slot_ref
  1.4 0.0 copy-start
  1.4 0.7 copy-done
  2.1 0.0 copy-start.1
  2.1 0.7 copy-done.1
  2.8 1.3 %shard_map.68 = (f32[1,4096]{1,0:T(1,128)S(1)}, f32[1,4096]{1,0:T(1,128)S(1)}, f32[32,128]{1,0:T(8,128)S(1)}) custom-call(s32[1,4096]{1,0:T(1,128)S(1)} %bitcast.4, s32[1,4096]{1,0:T(1,128)S(1)} %bitcast.5, s32[32,1]{1,0:T(8,128)S(1)} %copy.9.slot_ref), custom_call_target="tpu_custom_call" | custom-call | tf_op jit(solution)/shard_map/pallas_call | solution.py:49
  4.1 15.1 %shard_map.69 = (bf16[16,64,320]{2,1,0:T(8,128)(2,1)}, bf16[16,80,320]{2,1,0:T(8,128)(2,1)}) custom-call(bf16[128,4096]{1,0:T(8,128)(2,1)} %cov_ref.1, bf16[16,4096]{1,0:T(8,128)(2,1)} %pseudo_ref.1, f32[1,4096]{1,0:T(1,128)S(1)} %get-tuple-element.36.target_ref, f32[1,4096]{1,0:T(1,128)S(1)} %get-tuple-element.37.rank_ref, ...), custom_call_target="tpu_custom_call" | custom-call | tf_op jit(solution)/shard_map/pallas_call | solution.py:107
  19.2 6.2 %all-to-all-start.3 = ((bf16[16,64,320]{2,1,0:T(8,128)(2,1)}), bf16[16,64,320]{2,1,0:T(8,128)(2,1)S(1)}, u32[]{:S(2)}, u32[]{:S(2)}) async-start(bf16[16,64,320]{2,1,0:T(8,128)(2,1)} %get-tuple-element.39), calls=%async_computation.3 | async-start | bytes 1572864 | tf_op jit(solution)/shard_map/all_to_all | solution.py:274
  25.3 19.6 %all-to-all-done.3 = bf16[16,64,320]{2,1,0:T(8,128)(2,1)S(1)} async-done(((bf16[16,64,320]{2,1,0:T(8,128)(2,1)}), bf16[16,64,320]{2,1,0:T(8,128)(2,1)S(1)}, u32[]{:S(2)}, u32[]{:S(2)}) %all-to-all-start.3) | async-done | bytes 655392 | tf_op jit(solution)/shard_map/all_to_all | solution.py:274
  44.9 0.6 slice_reduce_fusion
  46.2 70.6 %conditional.1 = ((f32[2,17,128,256]{3,2,1,0:T(8,128)}, f32[2,256]{1,0:T(2,128)S(1)})) conditional(s32[]{:T(128)} %convert_element_type.3, (bf16[16,80,320]{2,1,0:T(8,128)(2,1)}, bf16[16,64,320]{2,1,0:T(8,128)(2,1)S(1)}) %tuple.14, (bf16[128,4096]{1,0:T(8,128)(2,1)}, bf16[16,4096]{1,0:T(8,128)(2,1)}, f32[1,4096]{1,0:T(1,128)S(1)}, ...), branch_computations={%region_1.0_spmd, %region_2.0_spmd} | conditional | flops 36507222016 | bytes 8388648 | solution.py:312
  46.2 4.6 %all-to-all-start = ((bf16[16,80,320]{2,1,0:T(8,128)(2,1)}), bf16[16,80,320]{2,1,0:T(8,128)(2,1)S(1)}, u32[]{:S(2)}, u32[]{:S(2)}) async-start(bf16[16,80,320]{2,1,0:T(8,128)(2,1)} %get-tuple-element.14), calls=%async_computation | async-start | bytes 1966080 | tf_op jit(solution)/shard_map/cond/branch_0_fun/all_to_all | solution.py:274
  50.8 24.8 %branch_0_fun.2 = (f32[2,17,128,256]{3,2,1,0:T(8,128)}, f32[2,256]{1,0:T(2,128)S(1)}) custom-call(bf16[16,64,320]{2,1,0:T(8,128)(2,1)S(1)} %get-tuple-element.15.refs_0_.refs_1_), custom_call_target="tpu_custom_call" | custom-call | flops 8556380160 | bytes 655360 | tf_op jit(solution)/shard_map/cond/branch_0_fun/pallas_call | solution.py:247
  75.7 0.0 all-to-all-done.refs_0_
  75.7 41.1 %branch_0_fun.3 = (f32[2,17,128,256]{3,2,1,0:T(8,128)}, f32[2,256]{1,0:T(2,128)S(1)}) custom-call(bf16[16,80,320]{2,1,0:T(8,128)(2,1)S(1)} %all-to-all-done.refs_0_, bf16[16,64,320]{2,1,0:T(8,128)(2,1)S(1)} %get-tuple-element.15.refs_0_.refs_1_, f32[2,17,128,256]{3,2,1,0:T(8,128)} %get-tuple-element.16.refs_2_, ...), custom_call_target="tpu_custom_call", output_to_operand_aliasing={{0}: (2, {})} | custom-call | flops 14260633600 | bytes 819200 | tf_op jit(solution)/shard_map/cond/branch_0_fun/pallas_call | solution.py:247
  116.8 0.1 reduce_max.19
  116.9 5.4 %pmax.7 = f32[2]{0:T(128)} all-reduce(f32[2]{0:T(128)S(1)} %reduce_max.19), channel_id=1, replica_groups=mesh['node'=16,'feat'=2] {'feat'}, use_global_device_ids=true, to_apply=%region_4.0 | all-reduce | flops 2 | bytes 16 | tf_op jit(solution)/shard_map/pmax | solution.py:315
Async XLA Ops:
  1.4 0.7 copy-start
  2.1 0.7 copy-start.1
  19.2 25.7 %all-to-all-start.3 = ((bf16[16,64,320]{2,1,0:T(8,128)(2,1)}), bf16[16,64,320]{2,1,0:T(8,128)(2,1)S(1)}, u32[]{:S(2)}, u32[]{:S(2)}) async-start(bf16[16,64,320]{2,1,0:T(8,128)(2,1)} %get-tuple-element.39), calls=%async_computation.3 | async-start | bytes 1572864 | tf_op jit(solution)/shard_map/all_to_all | solution.py:274
  46.2 29.5 %all-to-all-start = ((bf16[16,80,320]{2,1,0:T(8,128)(2,1)}), bf16[16,80,320]{2,1,0:T(8,128)(2,1)S(1)}, u32[]{:S(2)}, u32[]{:S(2)}) async-start(bf16[16,80,320]{2,1,0:T(8,128)(2,1)} %get-tuple-element.14), calls=%async_computation | async-start | bytes 1966080 | tf_op jit(solution)/shard_map/cond/branch_0_fun/all_to_all | solution.py:274

commit v3 on v2

--- a/solution.py
+++ b/solution.py
@@ -142,12 +142,10 @@
 
 def histogram_kernel(capacity, local, first, size, chained, *refs):
     if chained:
-        arrived, stats, _, before_ref, out_ref, best_ref, high, low, values = refs[:9]
-        sides = refs[9:]
+        arrived, stats, _, before_ref, out_ref, best_ref, high, low, values = refs
     else:
-        arrived, out_ref, best_ref, high, low, values = refs[:6]
+        arrived, out_ref, best_ref, high, low, values = refs
         stats = arrived
-        sides = refs[6:]
     group = pl.program_id(0)
     rows = high.shape[2]
 
@@ -178,13 +176,15 @@
     subf = sub.astype(jnp.float32)
     wanted = (sub % 4).astype(jnp.float32)
     zero, one = jnp.bfloat16(0), jnp.bfloat16(1)
+    tables = []
     for turn in range(2 * local):
         q, n = turn // local, turn % local
-        left_side, right_side = sides[2 * turn], sides[2 * turn + 1]
+        sums = None
         for c in range(rows // step):
             span = pl.ds(c * step, step)
             stat = values[n, :, span]
             mixed = None
+            left_side, right_side = [], []
             for f in range(4):
                 row = pl.ds(group * 8 + q * 4 + f, 1)
                 top = jnp.broadcast_to(high[n, row, span], (16, step))
@@ -192,14 +192,18 @@
                 mixed = top if f == 0 else jnp.where(sub >= 4 * f, top, mixed)
                 top = top.astype(jnp.bfloat16)
                 for h in range(HI):
-                    at = (f * HI + h) * 16
-                    left_side[at : at + 16, span] = jnp.where(top == jnp.bfloat16(h), stat, zero)
+                    left_side.append(jnp.where(top == jnp.bfloat16(h), stat, zero))
                 for j in range(LO // 16):
                     at = (subf + float(16 * j)).astype(jnp.bfloat16)
-                    right_side[f * LO + 16 * j : f * LO + 16 * j + 16, span] = jnp.where(bottom == at, one, zero)
-            left_side[256:272, span] = jnp.where(mixed == wanted, 1.0, 0.0).astype(jnp.bfloat16)
-        sums = lax.dot_general(left_side[...], right_side[...], NT, preferred_element_type=jnp.float32)
-        pieces = []
+                    right_side.append(jnp.where(bottom == at, one, zero))
+            left_side.append(jnp.where(mixed == wanted, 1.0, 0.0).astype(jnp.bfloat16))
+            product = lax.dot_general(
+                jnp.concatenate(left_side, axis=0),
+                jnp.concatenate(right_side, axis=0),
+                NT,
+                preferred_element_type=jnp.float32,
+            )
+            sums = product if sums is None else sums + product
         weights = []
         for f in range(4):
             lanes = slice(f * LO, (f + 1) * LO)
@@ -207,23 +211,26 @@
             weight = jnp.concatenate([sums[256 + f * HI + h : 257 + f * HI + h, lanes] for h in range(HI)], axis=1)
             out_ref[n, 0, q * 4 + f : q * 4 + f + 1, :] = weight
             out_ref[n, 1:17, q * 4 + f, :] = piece
-            pieces.append(piece)
+            tables.append(piece)
             weights.append(weight)
-        table = jnp.concatenate(pieces + weights + [jnp.zeros((4, B), jnp.float32)], axis=0)
-        one_part = table.astype(jnp.bfloat16)
-        table = table - one_part.astype(jnp.float32)
-        two_part = table.astype(jnp.bfloat16)
-        three_part = (table - two_part.astype(jnp.float32)).astype(jnp.bfloat16)
-        left = (
-            jnp.dot(three_part, upper, preferred_element_type=jnp.float32)
-            + jnp.dot(two_part, upper, preferred_element_type=jnp.float32)
-            + jnp.dot(one_part, upper, preferred_element_type=jnp.float32)
-        )
-        total = left[:, B - 1 : B]
-        right = total - left
+        tables.append(jnp.concatenate(weights + [jnp.zeros((4, B), jnp.float32)], axis=0))
+    table = jnp.concatenate(tables, axis=0)
+    one_part = table.astype(jnp.bfloat16)
+    table = table - one_part.astype(jnp.float32)
+    two_part = table.astype(jnp.bfloat16)
+    three_part = (table - two_part.astype(jnp.float32)).astype(jnp.bfloat16)
+    left = (
+        jnp.dot(three_part, upper, preferred_element_type=jnp.float32)
+        + jnp.dot(two_part, upper, preferred_element_type=jnp.float32)
+        + jnp.dot(one_part, upper, preferred_element_type=jnp.float32)
+    )
+    total = left[:, B - 1 : B]
+    right = total - left
+    for turn in range(2 * local):
+        n = turn % local
         for f in range(4):
-            span = slice(16 * f, 16 * f + 16)
-            count = slice(64 + f, 65 + f)
+            span = slice(72 * turn + 16 * f, 72 * turn + 16 * f + 16)
+            count = slice(72 * turn + 64 + f, 72 * turn + 65 + f)
             squared = lambda side: jnp.sum(side[span] * side[span], axis=0, keepdims=True) / (side[count] + 1.0)
             gain = squared(left) + squared(right) - squared(total)
             best_ref[n : n + 1, :] = jnp.maximum(best_ref[n : n + 1, :], gain)
@@ -260,8 +267,7 @@
             pltpu.VMEM((local, size, rows), jnp.float32),
             pltpu.VMEM((local, size, rows), jnp.float32),
             pltpu.VMEM((local, 16, rows), jnp.bfloat16),
-        ]
-        + [pltpu.VMEM((272, rows), jnp.bfloat16), pltpu.VMEM((256, rows), jnp.bfloat16)] * (2 * local),
+        ],
         input_output_aliases={2: 0} if chained else {},
         compiler_params=pltpu.CompilerParams(vmem_limit_bytes=VMEM),
         cost_estimate=pl.CostEstimate(
@@ -292,7 +298,7 @@
     nodes = node_slot.shape[0]
     local = nodes // devices
     most = 2 * rows // nodes
-    early = features // 8 * 3
+    early = features // 2
     early = early if early % 16 == 0 else features
     sizes = [16 + early] + ([features - early] if early < features else [])
     small = most - 96 if most % LANES == 0 and most > LANES else most

time: 124 us -> 98.5 us (0.79)
  Pallas kernels: 82.3 us -> 51.3 us
  waiting for transfers between devices: 19.6 us -> 25.9 us
    pallas_call x2, Pallas kernels: 65.9 us -> 34.9 us  [histogram_part(): pl.pallas_call(functools.partial(histogram_kernel, capacity, local, first...]
    all_to_all x2, waiting for transfers between devices: 19.6 us -> 25.9 us  [swap(): lax.all_to_all(block, 'node', split_axis=0, concat_axis=0, tiled=True)]
  transfers between devices with their start and end apart: 2 -> 2, of which waited for: 1 -> 2; matrix products, arithmetic and copies ran while one was open for 0% -> 0% of each run, Pallas kernels for 20% -> 18%
where the time goes in v3:
time: 98.5 us; the launch traced here: 97.7 us
  Pallas kernels  51.3 us (52%)
  waiting for transfers between devices  25.9 us (26%)
  starting transfers between devices  10.8 us (11%)
  blocking collectives  5.44 us (6%)
  local copies, waits for them, and re-layouts  2.17 us (2%)
  between operations  1.29 us (1%)
    pallas_call x2, Pallas kernels, histogram_part(): pl.pallas_call(functools.partial(histogram_kernel, capacity, local, first...  34.9 us
    all_to_all x2, waiting for transfers between devices, swap(): lax.all_to_all(block, 'node', split_axis=0, concat_axis=0, tiled=True)  25.9 us
    pallas_call x1, Pallas kernels, permute(): pl.pallas_call(functools.partial(permute_kernel, capacity, local, pair),...  15.1 us
    all_to_all x2, starting transfers between devices, swap(): lax.all_to_all(block, 'node', split_axis=0, concat_axis=0, tiled=True)  10.8 us
    pmax x1, blocking collectives, on_device(): best_gain = lax.pmax(jnp.max(best, axis=1), 'feat')  5.44 us
  transfers between devices with their start and end apart: 2, of which 2 were waited for; matrix products, arithmetic and copies ran while one was open for 0% of the time, Pallas kernels for 18%

profile of v3, /device:TPU:20, one launch (start us, length us, event | category | flops | bytes accessed | tf_op | source)
XLA Modules:
  0.0 97.7 jit_solution(4291470049787670010)
XLA Ops:
  0.6 0.7 copy.9.slot_ref
  1.4 0.0 copy-start
  1.4 0.7 copy-done
  2.1 0.0 copy-start.1
  2.1 0.7 copy-done.1
  2.8 1.3 %shard_map.68 = (f32[1,4096]{1,0:T(1,128)S(1)}, f32[1,4096]{1,0:T(1,128)S(1)}, f32[32,128]{1,0:T(8,128)S(1)}) custom-call(s32[1,4096]{1,0:T(1,128)S(1)} %bitcast.4, s32[1,4096]{1,0:T(1,128)S(1)} %bitcast.5, s32[32,1]{1,0:T(8,128)S(1)} %copy.9.slot_ref), custom_call_target="tpu_custom_call" | custom-call | tf_op jit(solution)/shard_map/pallas_call | solution.py:49
  4.1 15.1 %shard_map.69 = (bf16[16,80,320]{2,1,0:T(8,128)(2,1)}, bf16[16,64,320]{2,1,0:T(8,128)(2,1)}) custom-call(bf16[128,4096]{1,0:T(8,128)(2,1)} %cov_ref.1, bf16[16,4096]{1,0:T(8,128)(2,1)} %pseudo_ref.1, f32[1,4096]{1,0:T(1,128)S(1)} %get-tuple-element.36.target_ref, f32[1,4096]{1,0:T(1,128)S(1)} %get-tuple-element.37.rank_ref, ...), custom_call_target="tpu_custom_call" | custom-call | tf_op jit(solution)/shard_map/pallas_call | solution.py:107
  19.2 6.2 %all-to-all-start.3 = ((bf16[16,80,320]{2,1,0:T(8,128)(2,1)}), bf16[16,80,320]{2,1,0:T(8,128)(2,1)S(1)}, u32[]{:S(2)}, u32[]{:S(2)}) async-start(bf16[16,80,320]{2,1,0:T(8,128)(2,1)} %get-tuple-element.39), calls=%async_computation.3 | async-start | bytes 1966080 | tf_op jit(solution)/shard_map/all_to_all | solution.py:280
  25.4 23.8 %all-to-all-done.3 = bf16[16,80,320]{2,1,0:T(8,128)(2,1)S(1)} async-done(((bf16[16,80,320]{2,1,0:T(8,128)(2,1)}), bf16[16,80,320]{2,1,0:T(8,128)(2,1)S(1)}, u32[]{:S(2)}, u32[]{:S(2)}) %all-to-all-start.3) | async-done | bytes 819232 | tf_op jit(solution)/shard_map/all_to_all | solution.py:280
  49.1 0.6 slice_reduce_fusion
  50.4 41.7 %conditional.1 = ((f32[2,17,128,256]{3,2,1,0:T(8,128)}, f32[2,256]{1,0:T(2,128)S(1)})) conditional(s32[]{:T(128)} %convert_element_type.3, (bf16[16,64,320]{2,1,0:T(8,128)(2,1)}, bf16[16,80,320]{2,1,0:T(8,128)(2,1)S(1)}) %tuple.14, (bf16[128,4096]{1,0:T(8,128)(2,1)}, bf16[16,4096]{1,0:T(8,128)(2,1)}, f32[1,4096]{1,0:T(1,128)S(1)}, ...), branch_computations={%region_1.0_spmd, %region_2.0_spmd} | conditional | flops 36507222016 | bytes 8126504 | solution.py:318
  50.4 4.6 %all-to-all-start = ((bf16[16,64,320]{2,1,0:T(8,128)(2,1)}), bf16[16,64,320]{2,1,0:T(8,128)(2,1)S(1)}, u32[]{:S(2)}, u32[]{:S(2)}) async-start(bf16[16,64,320]{2,1,0:T(8,128)(2,1)} %get-tuple-element.14), calls=%async_computation | async-start | bytes 1572864 | tf_op jit(solution)/shard_map/cond/branch_0_fun/all_to_all | solution.py:280
  55.1 17.4 %branch_0_fun.2 = (f32[2,17,128,256]{3,2,1,0:T(8,128)}, f32[2,256]{1,0:T(2,128)S(1)}) custom-call(bf16[16,80,320]{2,1,0:T(8,128)(2,1)S(1)} %get-tuple-element.15.refs_0_.refs_1_), custom_call_target="tpu_custom_call" | custom-call | flops 11408506880 | bytes 819200 | tf_op jit(solution)/shard_map/cond/branch_0_fun/pallas_call | solution.py:254
  72.5 2.1 %all-to-all-done.refs_0_ = bf16[16,64,320]{2,1,0:T(8,128)(2,1)S(1)} async-done(((bf16[16,64,320]{2,1,0:T(8,128)(2,1)}), bf16[16,64,320]{2,1,0:T(8,128)(2,1)S(1)}, u32[]{:S(2)}, u32[]{:S(2)}) %all-to-all-start) | async-done | bytes 655392 | tf_op jit(solution)/shard_map/cond/branch_0_fun/all_to_all | solution.py:280
  74.6 17.5 %branch_0_fun.3 = (f32[2,17,128,256]{3,2,1,0:T(8,128)}, f32[2,256]{1,0:T(2,128)S(1)}) custom-call(bf16[16,64,320]{2,1,0:T(8,128)(2,1)S(1)} %all-to-all-done.refs_0_, bf16[16,80,320]{2,1,0:T(8,128)(2,1)S(1)} %get-tuple-element.15.refs_0_.refs_1_, f32[2,17,128,256]{3,2,1,0:T(8,128)} %get-tuple-element.16.refs_2_, ...), custom_call_target="tpu_custom_call", output_to_operand_aliasing={{0}: (2, {})} | custom-call | flops 11408506880 | bytes 655360 | tf_op jit(solution)/shard_map/cond/branch_0_fun/pallas_call | solution.py:254
  92.1 0.1 reduce_max.19
  92.2 5.4 %pmax.7 = f32[2]{0:T(128)} all-reduce(f32[2]{0:T(128)S(1)} %reduce_max.19), channel_id=1, replica_groups=mesh['node'=16,'feat'=2] {'feat'}, use_global_device_ids=true, to_apply=%region_4.0 | all-reduce | flops 2 | bytes 16 | tf_op jit(solution)/shard_map/pmax | solution.py:321
Async XLA Ops:
  1.4 0.7 copy-start
  2.1 0.7 copy-start.1
  19.2 29.9 %all-to-all-start.3 = ((bf16[16,80,320]{2,1,0:T(8,128)(2,1)}), bf16[16,80,320]{2,1,0:T(8,128)(2,1)S(1)}, u32[]{:S(2)}, u32[]{:S(2)}) async-start(bf16[16,80,320]{2,1,0:T(8,128)(2,1)} %get-tuple-element.39), calls=%async_computation.3 | async-start | bytes 1966080 | tf_op jit(solution)/shard_map/all_to_all | solution.py:280
  50.4 24.2 %all-to-all-start = ((bf16[16,64,320]{2,1,0:T(8,128)(2,1)}), bf16[16,64,320]{2,1,0:T(8,128)(2,1)S(1)}, u32[]{:S(2)}, u32[]{:S(2)}) async-start(bf16[16,64,320]{2,1,0:T(8,128)(2,1)} %get-tuple-element.14), calls=%async_computation | async-start | bytes 1572864 | tf_op jit(solution)/shard_map/cond/branch_0_fun/all_to_all | solution.py:280

commit v4 on v3

--- a/solution.py
+++ b/solution.py
@@ -23,42 +23,29 @@
     return jnp.where(row <= column, 1.0, 0.0).astype(jnp.bfloat16)
 
 
-def rank_kernel(honest_ref, destination_ref, slot_ref, target_ref, rank_ref, count_ref):
-    nodes = slot_ref.shape[0]
+def rank_rows(honest_ref, destination_ref, slot_ref, target_ref, rank_ref, count_ref):
+    nodes = slot_ref.shape[1]
     rows = honest_ref.shape[1]
     upper = triangle()
+    across = lax.broadcasted_iota(jnp.int32, (nodes, nodes), 0) == lax.broadcasted_iota(jnp.int32, (nodes, nodes), 1)
+    slots = jnp.sum(jnp.where(across, slot_ref[...].astype(jnp.float32), 0.0), axis=1, keepdims=True)
     index = lax.broadcasted_iota(jnp.int32, (nodes, B), 0)
     carry = jnp.zeros((nodes, 1), jnp.float32)
     for block in range(rows // B):
         span = pl.ds(block * B, B)
         named = destination_ref[:, span] == index
-        target = jnp.sum(jnp.where(named, slot_ref[...], 0), axis=0, keepdims=True)
+        target = jnp.sum(jnp.where(named, slots, 0.0), axis=0, keepdims=True)
         active = honest_ref[:, span] == 0
-        owned = jnp.where((target == index) & active, 1.0, 0.0)
+        owned = jnp.where((target == index.astype(jnp.float32)) & active, 1.0, 0.0)
         upto = jnp.dot(owned.astype(jnp.bfloat16), upper, preferred_element_type=jnp.float32) + carry
-        rank = jnp.sum(owned * upto, axis=0, keepdims=True) - 1.0
-        target_ref[:, span] = target.astype(jnp.float32)
-        rank_ref[:, span] = rank
+        target_ref[:, span] = target
+        rank_ref[:, span] = jnp.sum(owned * upto, axis=0, keepdims=True) - 1.0
         carry = upto[:, B - 1 : B]
     count_ref[...] = jnp.broadcast_to(carry, count_ref.shape)
 
 
-def ranks(honest, destination, node_slot):
-    rows = honest.shape[0]
-    nodes = node_slot.shape[0]
-    return pl.pallas_call(
-        rank_kernel,
-        out_shape=(
-            jax.ShapeDtypeStruct((1, rows), jnp.float32),
-            jax.ShapeDtypeStruct((1, rows), jnp.float32),
-            jax.ShapeDtypeStruct((nodes, LANES), jnp.float32),
-        ),
-        compiler_params=pltpu.CompilerParams(vmem_limit_bytes=VMEM),
-    )(honest.reshape(1, rows), destination.reshape(1, rows), node_slot.reshape(nodes, 1))
-
-
-def permute_kernel(capacity, local, pair, cov_ref, pseudo_ref, target_ref, rank_ref, count_ref, *rest):
-    outs, payload, places = rest[: -1 - pair * local], rest[-1 - pair * local], rest[-pair * local :]
+def permute_kernel(capacity, local, pair, cov_ref, pseudo_ref, honest_ref, destination_ref, slot_ref, *rest):
+    outs, (payload, target_ref, rank_ref, count_ref) = rest[:-4], rest[-4:]
     group = pl.program_id(0)
     rows = cov_ref.shape[1]
     head = capacity // LANES * LANES
@@ -69,38 +56,46 @@
         payload[0:16, :] = pseudo_ref[...]
         level = jnp.floor(cov_ref[...].astype(jnp.float32) * B) + 1.0
         payload[16:, :] = level.astype(jnp.bfloat16)
+        rank_rows(honest_ref, destination_ref, slot_ref, target_ref, rank_ref, count_ref)
 
     over = jnp.max(count_ref[...], axis=0, keepdims=True)[:, 0:1] > float(capacity)
     step = math.gcd(rows, 512)
-    for d in range(pair):
-        for n in range(local):
-            place = places[d * local + n]
-            node = ((group * pair + d) * local + n).astype(jnp.float32)
-            for c in range(rows // step):
-                span = pl.ds(c * step, step)
-                key = jnp.where(target_ref[:, span] == node, rank_ref[:, span], -1.0)
-                key = jnp.broadcast_to(key, (16, step)).astype(jnp.bfloat16)
-                for j in range(capacity // 16):
-                    at = lax.broadcasted_iota(jnp.int32, (16, step), 0).astype(jnp.float32) + float(16 * j)
-                    hit = jnp.where(key == at.astype(jnp.bfloat16), jnp.bfloat16(1), jnp.bfloat16(0))
-                    place[16 * j : 16 * j + 16, span] = hit
-            moved = lax.dot_general(payload[...], place[...], NT, preferred_element_type=jnp.float32)
-            first = 0
-            for out in outs:
-                size = out.shape[1]
-                part = moved[first : first + size]
-                if first == 0:
-                    part = jnp.where(over, POISON, part)
-                part = part.astype(jnp.bfloat16)
-                out[d, :, n * head : (n + 1) * head] = part[:, :head]
-                if tail:
-                    at = local * head + n * tail
-                    out[d, :, at : at + tail] = part[:, head:]
-                first += size
-
-
-def permute(covariates, pseudo, target, rank, count, capacity, local, devices, sizes):
+    sub = lax.broadcasted_iota(jnp.int32, (16, step), 0).astype(jnp.float32)
+    moved = None
+    for c in range(rows // step):
+        span = pl.ds(c * step, step)
+        target, rank = target_ref[:, span], rank_ref[:, span]
+        heads, tails = [], []
+        for i in range(pair * local):
+            node = (group * pair * local + i).astype(jnp.float32)
+            key = jnp.where(target == node, rank, -1.0)
+            key = jnp.broadcast_to(key, (16, step)).astype(jnp.bfloat16)
+            for j in range(capacity // 16):
+                at = (sub + float(16 * j)).astype(jnp.bfloat16)
+                hit = jnp.where(key == at, jnp.bfloat16(1), jnp.bfloat16(0))
+                (heads if 16 * j < head else tails).append(hit)
+        product = lax.dot_general(
+            payload[:, span], jnp.concatenate(heads + tails, axis=0), NT, preferred_element_type=jnp.float32
+        )
+        moved = product if moved is None else moved + product
+    first = 0
+    for out in outs:
+        size = out.shape[1]
+        part = moved[first : first + size]
+        if first == 0:
+            part = jnp.where(over, POISON, part)
+        part = part.astype(jnp.bfloat16)
+        for d in range(pair):
+            out[d, :, : local * head] = part[:, d * local * head : (d + 1) * local * head]
+            if tail:
+                at = pair * local * head + d * local * tail
+                out[d, :, local * head :] = part[:, at : at + local * tail]
+        first += size
+
+
+def permute(covariates, pseudo, honest, destination, node_slot, capacity, local, devices, sizes):
     features, rows = covariates.shape
+    nodes = node_slot.shape[0]
     width = local * capacity
     pair = 2 if devices % 2 == 0 else 1
     whole = lambda d: (0, 0)
@@ -112,14 +107,18 @@
             pl.BlockSpec((16, rows), whole),
             pl.BlockSpec((1, rows), whole),
             pl.BlockSpec((1, rows), whole),
-            pl.BlockSpec(count.shape, whole),
+            pl.BlockSpec((1, nodes), whole),
         ],
         out_specs=[pl.BlockSpec((pair, size, width), lambda d: (d, 0, 0)) for size in sizes],
         out_shape=[jax.ShapeDtypeStruct((devices, size, width), jnp.bfloat16) for size in sizes],
-        scratch_shapes=[pltpu.VMEM((features + 16, rows), jnp.bfloat16)]
-        + [pltpu.VMEM((capacity, rows), jnp.bfloat16)] * (pair * local),
+        scratch_shapes=[
+            pltpu.VMEM((features + 16, rows), jnp.bfloat16),
+            pltpu.VMEM((1, rows), jnp.float32),
+            pltpu.VMEM((1, rows), jnp.float32),
+            pltpu.VMEM((nodes, LANES), jnp.float32),
+        ],
         compiler_params=pltpu.CompilerParams(vmem_limit_bytes=VMEM),
-    )(covariates, pseudo, target, rank, count)
+    )(covariates, pseudo, honest.reshape(1, rows), destination.reshape(1, rows), node_slot.reshape(1, nodes))
 
 
 def gather_rows(arrived, first, size, node, capacity, local, store):
@@ -302,10 +301,9 @@
     early = early if early % 16 == 0 else features
     sizes = [16 + early] + ([features - early] if early < features else [])
     small = most - 96 if most % LANES == 0 and most > LANES else most
-    target, rank, count = ranks(honest, destination, node_slot)
 
     def route(capacity):
-        return permute(covariates, pseudo, target, rank, count, capacity, local, devices, sizes)
+        return permute(covariates, pseudo, honest, destination, node_slot, capacity, local, devices, sizes)
 
     def full():
         sent = route(most)

time: 98.5 us -> 97.4 us (0.989)
  local copies, waits for them, and re-layouts: 2.17 us -> 0 us
  Pallas kernels: 51.3 us -> 52.5 us
    pallas_call x1, Pallas kernels: 15.1 us -> 17.6 us  [permute(): pl.pallas_call(functools.partial(permute_kernel, capacity, local, pair),...]
    unnamed x4 -> x0, local copies, waits for them, and re-layouts: 1.43 us -> none
    pallas_call x1 -> x0, Pallas kernels: 1.32 us -> none  [ranks(): pl.pallas_call(rank_kernel, out_shape=(jax.ShapeDtypeStruct((1, rows), jn...]
where the time goes in v4:
time: 97.4 us; the launch traced here: 96.7 us
  Pallas kernels  52.5 us (54%)
  waiting for transfers between devices  25.9 us (27%)
  starting transfers between devices  10.8 us (11%)
  blocking collectives  5.44 us (6%)
  between operations  1.29 us (1%)
    pallas_call x2, Pallas kernels, histogram_part(): pl.pallas_call(functools.partial(histogram_kernel, capacity, local, first...  34.9 us
    all_to_all x2, waiting for transfers between devices, swap(): lax.all_to_all(block, 'node', split_axis=0, concat_axis=0, tiled=True)  25.9 us
    pallas_call x1, Pallas kernels, permute(): pl.pallas_call(functools.partial(permute_kernel, capacity, local, pair),...  17.6 us
    all_to_all x2, starting transfers between devices, swap(): lax.all_to_all(block, 'node', split_axis=0, concat_axis=0, tiled=True)  10.8 us
    pmax x1, blocking collectives, on_device(): best_gain = lax.pmax(jnp.max(best, axis=1), 'feat')  5.44 us
  transfers between devices with their start and end apart: 2, of which 2 were waited for; matrix products, arithmetic and copies ran while one was open for 0% of the time, Pallas kernels for 18%

profile of v4, /device:TPU:20, one launch (start us, length us, event | category | flops | bytes accessed | tf_op | source)
XLA Modules:
  0.0 96.7 jit_solution(16313966919367681712)
XLA Ops:
  0.6 17.6 %shard_map.68 = (bf16[16,80,320]{2,1,0:T(8,128)(2,1)}, bf16[16,64,320]{2,1,0:T(8,128)(2,1)}) custom-call(bf16[128,4096]{1,0:T(8,128)(2,1)} %cov_ref.1, bf16[16,4096]{1,0:T(8,128)(2,1)} %pseudo_ref.1, s32[1,4096]{1,0:T(1,128)} %bitcast.7, s32[1,4096]{1,0:T(1,128)} %bitcast.9, s32[1,32]{1,0:T(1,128)} %bitcast.11), custom_call_target="tpu_custom_call" | custom-call | tf_op jit(solution)/shard_map/pallas_call | solution.py:102
  18.2 6.2 %all-to-all-start.3 = ((bf16[16,80,320]{2,1,0:T(8,128)(2,1)}), bf16[16,80,320]{2,1,0:T(8,128)(2,1)S(1)}, u32[]{:S(2)}, u32[]{:S(2)}) async-start(bf16[16,80,320]{2,1,0:T(8,128)(2,1)} %get-tuple-element.33), calls=%async_computation.3 | async-start | bytes 1966080 | tf_op jit(solution)/shard_map/all_to_all | solution.py:279
  24.4 23.8 %all-to-all-done.3 = bf16[16,80,320]{2,1,0:T(8,128)(2,1)S(1)} async-done(((bf16[16,80,320]{2,1,0:T(8,128)(2,1)}), bf16[16,80,320]{2,1,0:T(8,128)(2,1)S(1)}, u32[]{:S(2)}, u32[]{:S(2)}) %all-to-all-start.3) | async-done | bytes 819232 | tf_op jit(solution)/shard_map/all_to_all | solution.py:279
  48.1 0.6 slice_reduce_fusion
  49.4 41.7 %conditional.1 = ((f32[2,17,128,256]{3,2,1,0:T(8,128)}, f32[2,256]{1,0:T(2,128)S(1)})) conditional(s32[]{:T(128)} %convert_element_type.3, (bf16[16,64,320]{2,1,0:T(8,128)(2,1)}, bf16[16,80,320]{2,1,0:T(8,128)(2,1)S(1)}) %tuple.14, (s32[4096]{0:T(1024)}, s32[4096,1]{0,1:T(1,128)}, s32[32]{0:T(128)}, bf16[128,4096]{1,0:T(8,128)(2,1)}, ...), branch_computations={%region_1.0_spmd, %region_2.0_spmd} | conditional | flops 36507222016 | bytes 8126504 | solution.py:316
  49.4 4.6 %all-to-all-start = ((bf16[16,64,320]{2,1,0:T(8,128)(2,1)}), bf16[16,64,320]{2,1,0:T(8,128)(2,1)S(1)}, u32[]{:S(2)}, u32[]{:S(2)}) async-start(bf16[16,64,320]{2,1,0:T(8,128)(2,1)} %get-tuple-element.14), calls=%async_computation | async-start | bytes 1572864 | tf_op jit(solution)/shard_map/cond/branch_0_fun/all_to_all | solution.py:279
  54.1 17.5 %branch_0_fun.2 = (f32[2,17,128,256]{3,2,1,0:T(8,128)}, f32[2,256]{1,0:T(2,128)S(1)}) custom-call(bf16[16,80,320]{2,1,0:T(8,128)(2,1)S(1)} %get-tuple-element.15.refs_0_.refs_1_), custom_call_target="tpu_custom_call" | custom-call | flops 11408506880 | bytes 819200 | tf_op jit(solution)/shard_map/cond/branch_0_fun/pallas_call | solution.py:253
  71.5 2.1 %all-to-all-done.refs_0_ = bf16[16,64,320]{2,1,0:T(8,128)(2,1)S(1)} async-done(((bf16[16,64,320]{2,1,0:T(8,128)(2,1)}), bf16[16,64,320]{2,1,0:T(8,128)(2,1)S(1)}, u32[]{:S(2)}, u32[]{:S(2)}) %all-to-all-start) | async-done | bytes 655392 | tf_op jit(solution)/shard_map/cond/branch_0_fun/all_to_all | solution.py:279
  73.6 17.5 %branch_0_fun.3 = (f32[2,17,128,256]{3,2,1,0:T(8,128)}, f32[2,256]{1,0:T(2,128)S(1)}) custom-call(bf16[16,64,320]{2,1,0:T(8,128)(2,1)S(1)} %all-to-all-done.refs_0_, bf16[16,80,320]{2,1,0:T(8,128)(2,1)S(1)} %get-tuple-element.15.refs_0_.refs_1_, f32[2,17,128,256]{3,2,1,0:T(8,128)} %get-tuple-element.16.refs_2_, ...), custom_call_target="tpu_custom_call", output_to_operand_aliasing={{0}: (2, {})} | custom-call | flops 11408506880 | bytes 655360 | tf_op jit(solution)/shard_map/cond/branch_0_fun/pallas_call | solution.py:253
  91.1 0.1 reduce_max.19
  91.2 5.4 %pmax.7 = f32[2]{0:T(128)} all-reduce(f32[2]{0:T(128)S(1)} %reduce_max.19), channel_id=1, replica_groups=mesh['node'=16,'feat'=2] {'feat'}, use_global_device_ids=true, to_apply=%region_4.0 | all-reduce | flops 2 | bytes 16 | tf_op jit(solution)/shard_map/pmax | solution.py:319
Async XLA Ops:
  18.2 29.9 %all-to-all-start.3 = ((bf16[16,80,320]{2,1,0:T(8,128)(2,1)}), bf16[16,80,320]{2,1,0:T(8,128)(2,1)S(1)}, u32[]{:S(2)}, u32[]{:S(2)}) async-start(bf16[16,80,320]{2,1,0:T(8,128)(2,1)} %get-tuple-element.33), calls=%async_computation.3 | async-start | bytes 1966080 | tf_op jit(solution)/shard_map/all_to_all | solution.py:279
  49.4 24.2 %all-to-all-start = ((bf16[16,64,320]{2,1,0:T(8,128)(2,1)}), bf16[16,64,320]{2,1,0:T(8,128)(2,1)S(1)}, u32[]{:S(2)}, u32[]{:S(2)}) async-start(bf16[16,64,320]{2,1,0:T(8,128)(2,1)} %get-tuple-element.14), calls=%async_computation | async-start | bytes 1572864 | tf_op jit(solution)/shard_map/cond/branch_0_fun/all_to_all | solution.py:279
